TPU v7x, 32 devices: a whole 2x2x4 slice. The times are simulated.
32 devices in a mesh: tm: 16 (over z, y, core), col: 2 (over x).
Axes of the slice: x: 2, y: 2, z: 4, core: 2. Of those that a mesh axis runs over, the one named last changes fastest.
Arguments:
- design: bfloat16 [2048, 2, 512], P('tm', None, 'col'), may hold values from -512 to 512
- filter_taps: bfloat16 [16, 2, 512], replicated, may hold values from -3 to 3
- segment: int32 [2048], P('tm'), may hold values from 0 to 15, never falling along the last dimension, each value on 1 to 256 neighbouring positions
- valid_flags: int32 [2048], P('tm'), may hold values 0 or 1
- weights: float32 [2, 2048], P(None, 'tm'), may hold values from 0.05 to 20
- block_ids: int32 [2], replicated, may hold values from 0 to 1, each once
Outputs:
- normals: float32 [512, 512], P('tm', 'col')
All inputs are finite; a program needn't handle non-finite values. No bound on the sum of `valid_flags` on one device may be relied on, other than what follows from the above.
Results may differ from a plain program's by a relative error of at most 0.0013.
Values may be sent and summed in bfloat16 or wider, within the bound.
No kernel may reach another device: no remote copies, remote signals or barrier semaphores. Data moves between devices by JAX's collectives and lax.ppermute only.
A program may use at most 64 MiB of HBM per device.

v0:
```python
import jax
import jax.numpy as jnp
from jax import lax
from jax.sharding import PartitionSpec as P


def from_behind(x, axis, by):
    devices = lax.axis_size(axis)
    pairs = [(i, i + by) for i in range(devices) if 0 <= i + by < devices]
    return lax.ppermute(x, axis, pairs)


def body(design, filter_taps, segment, valid_flags, weights, block_ids):
    row_count = design.shape[0]
    block_width = design.shape[2]
    tap_count = filter_taps.shape[2]
    seg_count = filter_taps.shape[0]
    block_count = block_ids.shape[0]
    halo_depth = (tap_count - 2) // row_count + 1
    window_rows = (halo_depth + 1) * row_count
    selector = (segment[:, None] == jnp.arange(seg_count, dtype=jnp.int32)[None, :]).astype(
        jnp.bfloat16
    )
    tap_rows = jnp.einsum(
        "ts,skj->ktj", selector, filter_taps, preferred_element_type=jnp.float32
    ).astype(jnp.bfloat16)
    reversed_taps = tap_rows[:, :, ::-1]
    offset = window_rows - row_count - tap_count + 1
    padded = jnp.pad(
        reversed_taps, ((0, 0), (0, 0), (offset, window_rows + 1 - offset - tap_count))
    )
    toeplitz = padded.reshape(2, row_count * (window_rows + 1))[
        :, : row_count * window_rows
    ].reshape(2, row_count, window_rows)
    pieces = []
    for hop_index in range(halo_depth):
        pieces.append(from_behind(design, "tm", halo_depth - hop_index))
    earlier = jnp.concatenate(pieces, axis=0)
    own_part = jnp.einsum(
        "kts,skc->tkc",
        toeplitz[:, :, halo_depth * row_count :],
        design,
        preferred_element_type=jnp.float32,
    )
    past_part = jnp.einsum(
        "kts,skc->tkc",
        toeplitz[:, :, : halo_depth * row_count],
        earlier,
        preferred_element_type=jnp.float32,
    )
    filtered = (own_part + past_part).astype(jnp.bfloat16)
    row_weight = (weights * valid_flags[None, :].astype(jnp.float32)).T
    owner = block_ids[:, None] == jnp.arange(block_count, dtype=jnp.int32)[None, :]
    column = lax.axis_index("col")
    gathered = lax.all_gather(filtered, "col", axis=2, tiled=True)
    ordered = (
        jnp.einsum(
            "tkdc,dp->tkpc",
            gathered.reshape(row_count, 2, block_count, block_width),
            owner.astype(jnp.bfloat16),
            preferred_element_type=jnp.float32,
        )
        .astype(jnp.bfloat16)
        .reshape(row_count, 2, block_count * block_width)
    )
    own_cols = lax.dynamic_slice_in_dim(ordered, column * block_width, block_width, 2)
    scaled = (own_cols.astype(jnp.float32) * row_weight[:, :, None]).astype(jnp.bfloat16)
    summed = lax.psum_scatter(
        jnp.einsum("tkp,tkq->pq", ordered, scaled, preferred_element_type=jnp.float32),
        "tm",
        scatter_dimension=0,
        tiled=True,
    )
    return summed / (2.0 * row_count * lax.axis_size("tm"))


def solution(mesh):
    return jax.shard_map(
        body,
        mesh=mesh,
        in_specs=(P("tm", None, "col"), P(), P("tm"), P("tm"), P(None, "tm"), P()),
        out_specs=P("tm", "col"),
        check_vma=False,
    )
```

profile of v0, /device:TPU:0, one launch (start us, length us, event | category | flops | bytes accessed | tf_op | source)
XLA Modules:
  0.0 98.0 jit_solution(15735949541265817054)
XLA Ops:
  6.5 0.0 copy-start
  6.5 0.0 reduce-scatter.2.cloned.1.call-start
  6.5 1.0 %copy.19 = bf16[128,2,256]{0,2,1:T(8,128)(2,1)S(1)} copy(bf16[128,2,256]{2,1,0:T(2,128)(2,1)} %param.6) | data formatting | bytes 262144 | tf_op args[0]
  7.6 0.0 copy-start.2
  7.6 4.9 %collective-permute-start = (bf16[128,2,256]{0,2,1:T(8,128)(2,1)S(1)}, bf16[128,2,256]{0,2,1:T(8,128)(2,1)S(1)}, u32[]{:S(2)}, u32[]{:S(2)}) collective-permute-start(bf16[128,2,256]{0,2,1:T(8,128)(2,1)S(1)} %copy.19), channel_id=1, source_target_pairs={{0,8},{2,10},{4,12},{6,14},{8,16},{10,18},{12,20},{14,22},{16,24},... | collective-permute-start | bytes 393224 | tf_op jit(solution)/shard_map/ppermute | solution.py:10
  12.5 2.6 %collective-permute-start.1 = (bf16[128,2,256]{0,2,1:T(8,128)(2,1)S(1)}, bf16[128,2,256]{0,2,1:T(8,128)(2,1)S(1)}, u32[]{:S(2)}, u32[]{:S(2)}) collective-permute-start(bf16[128,2,256]{0,2,1:T(8,128)(2,1)S(1)} %copy.19), channel_id=1, source_target_pairs={{0,6},{2,8},{4,10},{6,12},{8,14},{10,16},{12,18},{14,20},{16,22},{... | collective-permute-start | bytes 393224 | tf_op jit(solution)/shard_map/ppermute | solution.py:10
  15.1 3.4 %collective-permute-start.2 = (bf16[128,2,256]{0,2,1:T(8,128)(2,1)S(1)}, bf16[128,2,256]{0,2,1:T(8,128)(2,1)S(1)}, u32[]{:S(2)}, u32[]{:S(2)}) collective-permute-start(bf16[128,2,256]{0,2,1:T(8,128)(2,1)S(1)} %copy.19), channel_id=1, source_target_pairs={{0,4},{2,6},{4,8},{6,10},{8,12},{10,14},{12,16},{14,18},{16,20},{1... | collective-permute-start | bytes 393224 | tf_op jit(solution)/shard_map/ppermute | solution.py:10
  18.6 2.6 %collective-permute-start.3 = (bf16[128,2,256]{0,2,1:T(8,128)(2,1)S(1)}, bf16[128,2,256]{0,2,1:T(8,128)(2,1)S(1)}, u32[]{:S(2)}, u32[]{:S(2)}) collective-permute-start(bf16[128,2,256]{0,2,1:T(8,128)(2,1)S(1)} %copy.19), channel_id=1, source_target_pairs={{0,2},{2,4},{4,6},{6,8},{8,10},{10,12},{12,14},{14,16},{16,18},{18... | collective-permute-start | bytes 393224 | tf_op jit(solution)/shard_map/ppermute | solution.py:10
  21.2 0.3 fusion
  21.5 0.8 rev.3
  22.4 0.2 pad.4
  22.5 1.1 %reshape.17 = bf16[2,82048]{1,0:T(2,128)(2,1)S(1)} reshape(bf16[2,128,641]{2,1,0:T(8,128)(2,1)S(1)} %pad.4) | data formatting | bytes 656384 | tf_op jit(solution)/shard_map/reshape | solution.py:32
  23.6 0.2 slice.12
  23.9 0.2 convolution_bitcast_fusion.2
  24.1 0.0 copy-start.3
  24.1 0.6 copy-done.3
  24.8 0.7 copy-done.1
  25.4 0.0 collective-permute-done
  25.4 0.0 collective-permute-done.1
  25.4 0.0 collective-permute-done.2
  25.5 0.0 collective-permute-done.3
  25.5 0.3 fusion.3
  25.8 7.0 %all_gather.3 = bf16[128,2,512]{2,0,1:T(8,128)(2,1)S(1)} all-gather(bf16[128,2,256]{2,0,1:T(8,128)(2,1)S(1)} %fusion.3), channel_id=1, replica_groups=mesh['tm'=16,'col'=2] {'col'}, dimensions={2}, use_global_device_ids=true | all-gather | bytes 393216 | tf_op jit(solution)/shard_map/all_gather | solution.py:55
  32.8 0.1 reshape.19
  32.8 0.6 copy-done.4
  33.4 0.4 fusion.1
  33.8 0.2 reshape.20
  34.0 0.1 constant_dynamic-slice_fusion
  34.1 1.1 %convolution_bitcast_fusion = f32[512,256]{1,0:T(8,128)} fusion(bf16[128,2,512]{2,1,0:T(2,128)(2,1)S(1)} %reshape.20, bf16[128,2,256]{2,1,0:T(2,128)(2,1)S(1)} %constant_dynamic-slice_fusion, f32[128,2]{0,1:T(2,128)S(1)} %multiply_bitcast_fusion), kind=kOutput, calls=%fused_computation | convolution fusion | flops 67305472 | bytes 918528 | tf_op jit(solution)/shard_map/tkp,tkq->pq/dot_general | solution.py:69
  35.2 0.0 reduce-scatter.2.cloned.1.call-update
  35.3 54.5 %reduce-scatter.2.cloned.1.call-done = f32[32,256]{1,0:T(8,128)} async-done(((f32[512,256]{1,0:T(8,128)}), f32[32,256]{1,0:T(8,128)}) %reduce-scatter.2.cloned.1.call-update) | async-done | bytes 32784 | tf_op jit(solution)/shard_map/reduce_scatter | solution.py:68
  89.8 1.4 %broadcast_multiply_fusion = f32[32,256]{1,0:T(8,128)} fusion(f32[32,256]{1,0:T(8,128)} %reduce-scatter.2.cloned.1.call-done), kind=kLoop, calls=%fused_computation.25 | loop fusion | flops 8192 | bytes 65536 | tf_op jit(solution)/shard_map/div | solution.py:74
  (7 shorter events, 0.1 us)
Async XLA Ops:
  6.5 14.7 %copy-start = (bf16[16,2,512]{2,1,0:T(2,128)(2,1)S(1)}, bf16[16,2,512]{2,1,0:T(2,128)(2,1)}, u32[]{:S(2)}) copy-start(bf16[16,2,512]{2,1,0:T(2,128)(2,1)} %param.7) | copy-start | bytes 98308
  6.5 83.2 %reduce-scatter.2.cloned.1.call-start = ((), (), s32[]{:S(2)}) async-start(), calls=%async_computation.1 | async-start | bytes 557056 | tf_op jit(solution)/shard_map/reduce_scatter | solution.py:68
  7.6 13.7 %copy-start.2 = (s32[128]{0:T(128)S(1)}, s32[128]{0:T(128)}, u32[]{:S(2)}) copy-start(s32[128]{0:T(128)} %param.8) | copy-start | bytes 1540
  7.6 17.8 %collective-permute-start = (bf16[128,2,256]{0,2,1:T(8,128)(2,1)S(1)}, bf16[128,2,256]{0,2,1:T(8,128)(2,1)S(1)}, u32[]{:S(2)}, u32[]{:S(2)}) collective-permute-start(bf16[128,2,256]{0,2,1:T(8,128)(2,1)S(1)} %copy.19), channel_id=1, source_target_pairs={{0,8},{2,10},{4,12},{6,14},{8,16},{10,18},{12,20},{14,22},{16,24},... | collective-permute-start | bytes 393224 | tf_op jit(solution)/shard_map/ppermute | solution.py:10
  12.5 12.9 %collective-permute-start.1 = (bf16[128,2,256]{0,2,1:T(8,128)(2,1)S(1)}, bf16[128,2,256]{0,2,1:T(8,128)(2,1)S(1)}, u32[]{:S(2)}, u32[]{:S(2)}) collective-permute-start(bf16[128,2,256]{0,2,1:T(8,128)(2,1)S(1)} %copy.19), channel_id=1, source_target_pairs={{0,6},{2,8},{4,10},{6,12},{8,14},{10,16},{12,18},{14,20},{16,22},{... | collective-permute-start | bytes 393224 | tf_op jit(solution)/shard_map/ppermute | solution.py:10
  15.1 10.3 %collective-permute-start.2 = (bf16[128,2,256]{0,2,1:T(8,128)(2,1)S(1)}, bf16[128,2,256]{0,2,1:T(8,128)(2,1)S(1)}, u32[]{:S(2)}, u32[]{:S(2)}) collective-permute-start(bf16[128,2,256]{0,2,1:T(8,128)(2,1)S(1)} %copy.19), channel_id=1, source_target_pairs={{0,4},{2,6},{4,8},{6,10},{8,12},{10,14},{12,16},{14,18},{16,20},{1... | collective-permute-start | bytes 393224 | tf_op jit(solution)/shard_map/ppermute | solution.py:10
  18.6 6.9 %collective-permute-start.3 = (bf16[128,2,256]{0,2,1:T(8,128)(2,1)S(1)}, bf16[128,2,256]{0,2,1:T(8,128)(2,1)S(1)}, u32[]{:S(2)}, u32[]{:S(2)}) collective-permute-start(bf16[128,2,256]{0,2,1:T(8,128)(2,1)S(1)} %copy.19), channel_id=1, source_target_pairs={{0,2},{2,4},{4,6},{6,8},{8,10},{10,12},{12,14},{14,16},{16,18},{18... | collective-permute-start | bytes 393224 | tf_op jit(solution)/shard_map/ppermute | solution.py:10
  24.1 0.7 copy-start.3
  24.7 0.7 copy-start.1
  32.8 0.7 copy-start.4
Sparse Core Ops, SparseCore 0:
  35.4 54.3 reduce-scatter.1
where the time goes:
time: 98.3 us; the launch traced here: 98 us
  waiting for transfers between devices  54.5 us (55%)
  starting transfers between devices  13.6 us (14%)
  between operations  13.6 us (14%)
  blocking collectives  6.98 us (7%)
  local copies, waits for them, and re-layouts  5.63 us (6%)
  matrix products  2.3 us (2%)
  other arithmetic  1.38 us (1%)
    reduce_scatter x1, waiting for transfers between devices, body(): lax.psum_scatter(jnp.einsum('tkp,tkq->pq', ordered, scaled, preferred_ele...  54.5 us
    ppermute x4, starting transfers between devices, from_behind(): return lax.ppermute(x, axis, pairs)  13.6 us
    all_gather x1, blocking collectives, body(): gathered = lax.all_gather(filtered, 'col', axis=2, tiled=True)  6.98 us
    unnamed x12, local copies, waits for them, and re-layouts  3 us
  transfers between devices with their start and end apart: 5, of which 1 were waited for; matrix products, arithmetic and copies ran while one was open for 3% of the time, Pallas kernels for 0%

commit v1 on v0

v1 whole, which is shorter than its diff:
```python
import jax
import jax.numpy as jnp
from jax import lax
from jax.sharding import PartitionSpec as P


def body(design, filter_taps, segment, valid_flags, weights, block_ids):
    row_count = design.shape[0]
    block_width = design.shape[2]
    tap_count = filter_taps.shape[2]
    seg_count = filter_taps.shape[0]
    block_count = block_ids.shape[0]
    devices = lax.axis_size("tm")
    columns = lax.axis_size("col")
    halo_depth = (tap_count - 2) // row_count + 1
    odd = lax.axis_index("tm") % 2 == 1
    swap = [(i, i ^ 1) for i in range(devices)]

    blocks = [design] + [None] * halo_depth
    for hop in range(2, halo_depth + 1, 2):
        blocks[hop] = lax.ppermute(design, "tm", [(i, i + hop) for i in range(devices - hop)])
    for hop in range(1, halo_depth + 1, 2):
        after = blocks[hop + 1] if hop + 1 <= halo_depth else blocks[hop - 1]
        blocks[hop] = lax.ppermute(jnp.where(odd, after, blocks[hop - 1]), "tm", swap)

    selector = (segment[:, None] == jnp.arange(seg_count, dtype=jnp.int32)[None, :]).astype(jnp.bfloat16)
    window_rows = (halo_depth + 1) * row_count
    tap_rows = jnp.einsum("ts,skj->ktj", selector, filter_taps, preferred_element_type=jnp.float32).astype(jnp.bfloat16)
    reversed_taps = tap_rows[:, :, ::-1]
    offset = window_rows - row_count - tap_count + 1
    padded = jnp.pad(reversed_taps, ((0, 0), (0, 0), (offset, window_rows + 1 - offset - tap_count)))
    toeplitz = padded.reshape(2, row_count * (window_rows + 1))[:, : row_count * window_rows].reshape(
        2, row_count, window_rows
    )
    filtered = sum(
        jnp.einsum(
            "kts,skc->ktc",
            toeplitz[:, :, (halo_depth - d) * row_count : (halo_depth - d + 1) * row_count],
            blocks[d],
            preferred_element_type=jnp.float32,
        )
        for d in range(halo_depth, -1, -1)
    ).astype(jnp.bfloat16)

    column = lax.axis_index("col")
    held = [filtered]
    for d in range(1, columns):
        held.append(lax.ppermute(filtered, "col", [((c + d) % columns, c) for c in range(columns)]))
    ids = [block_ids[(column + d) % columns] for d in range(columns)]

    def of_parameter(p):
        found = held[0]
        for d in range(1, columns):
            found = jnp.where(ids[d] == p, held[d], found)
        return found

    ordered = jnp.concatenate([of_parameter(p) for p in range(columns)], axis=2)
    row_weight = (weights * valid_flags[None, :].astype(jnp.float32))
    scaled = (of_parameter(column).astype(jnp.float32) * row_weight[:, :, None]).astype(jnp.bfloat16)
    total = jnp.einsum("ktp,ktq->pq", ordered, scaled, preferred_element_type=jnp.float32)
    total = total * (1.0 / (2.0 * row_count * devices))
    parts = total.reshape(devices // 2, 2, -1, block_width)
    even_part, odd_part = parts[:, 0], parts[:, 1]
    mine = jnp.where(odd, odd_part, even_part)
    other = jnp.where(odd, even_part, odd_part)
    mine = mine + lax.ppermute(other, "tm", swap)
    groups = [[2 * c + p for c in range(devices // 2)] for p in range(2)]
    return lax.all_to_all(mine, "tm", 0, 0, axis_index_groups=groups).sum(0)


def solution(mesh):
    return jax.shard_map(
        body,
        mesh=mesh,
        in_specs=(P("tm", None, "col"), P(), P("tm"), P("tm"), P(None, "tm"), P()),
        out_specs=P("tm", "col"),
        check_vma=False,
    )
```

time: 98.3 us -> 40.5 us (0.41)
  waiting for transfers between devices: 54.5 us -> 6.43 us
  between operations: 13.6 us -> 2.2 us
  blocking collectives: 6.98 us -> 12.9 us
  starting transfers between devices: 13.6 us -> 10.6 us
    reduce_scatter x1 -> x0, waiting for transfers between devices: 54.5 us -> none  [body(): lax.psum_scatter(jnp.einsum('tkp,tkq->pq', ordered, scaled, preferred_ele...]
    all_to_all x0 -> x1, blocking collectives: none -> 12.9 us  [body(): return lax.all_to_all(mine, 'tm', 0, 0, axis_index_groups=groups).sum(0)]
    all_gather x1 -> x0, blocking collectives: 6.98 us -> none  [body(): gathered = lax.all_gather(filtered, 'col', axis=2, tiled=True)]
    ppermute x4 -> x6, waiting for transfers between devices: 0.01 us -> 6.43 us  [the longest x1 4.22 us: body(): lax.ppermute(filtered, 'col', [((c + d) % columns, c) for c in range(colu...]
    ppermute x4 -> x6, starting transfers between devices: 13.6 us -> 10.6 us  [the longest x2 8.37 us: body(): lax.ppermute(design, 'tm', [(i, i + hop) for i in range(devices - hop)])]
    div x1 -> x0, other arithmetic: 1.37 us -> none  [body(): return summed / (2.0 * row_count * lax.axis_size('tm'))]
    dot_general x4 -> x6, matrix products: 2.03 us -> 1.18 us  [the longest x5 0.85 us: body(): jnp.einsum('kts,skc->ktc', toeplitz[:, :, (halo_depth - d) * row_count:(h...]
    unnamed x12 -> x14, local copies, waits for them, and re-layouts: 3 us -> 3.12 us
  transfers between devices with their start and end apart: 5 -> 6, of which waited for: 1 -> 3; matrix products, arithmetic and copies ran while one was open for 3% -> 9% of each run, Pallas kernels for 0% -> 0%
where the time goes in v1:
time: 40.5 us; the launch traced here: 40.3 us
  blocking collectives  12.9 us (32%)
  starting transfers between devices  10.6 us (26%)
  waiting for transfers between devices  6.43 us (16%)
  local copies, waits for them, and re-layouts  5.99 us (15%)
  between operations  2.2 us (5%)
  matrix products  1.44 us (4%)
  other arithmetic  0.78 us (2%)
    all_to_all x1, blocking collectives, body(): return lax.all_to_all(mine, 'tm', 0, 0, axis_index_groups=groups).sum(0)  12.9 us
    ppermute x2, starting transfers between devices, body(): lax.ppermute(design, 'tm', [(i, i + hop) for i in range(devices - hop)])  8.37 us
    ppermute x1, waiting for transfers between devices, body(): lax.ppermute(filtered, 'col', [((c + d) % columns, c) for c in range(colu...  4.22 us
    unnamed x14, local copies, waits for them, and re-layouts  3.12 us
    ppermute x1, starting transfers between devices, body(): lax.ppermute(filtered, 'col', [((c + d) % columns, c) for c in range(colu...  1.56 us
    ppermute x1, waiting for transfers between devices, body(): mine = mine + lax.ppermute(other, 'tm', swap)  1.52 us
    reshape x1, local copies, waits for them, and re-layouts, body(): padded.reshape(2, row_count * (window_rows + 1))  1.06 us
    dot_general x5, matrix products, body(): jnp.einsum('kts,skc->ktc', toeplitz[:, :, (halo_depth - d) * row_count:(h...  0.85 us
  transfers between devices with their start and end apart: 6, of which 3 were waited for; matrix products, arithmetic and copies ran while one was open for 9% of the time, Pallas kernels for 0%

profile of v1, /device:TPU:0, one launch (start us, length us, event | category | flops | bytes accessed | tf_op | source)
XLA Modules:
  0.0 40.3 jit_solution(18121693325597003154)
XLA Ops:
  0.0 0.9 %copy.18 = bf16[128,2,256]{2,0,1:T(8,128)(2,1)S(1)} copy(bf16[128,2,256]{2,1,0:T(2,128)(2,1)} %param.6) | data formatting | bytes 262144 | tf_op args[0]
  0.9 4.9 %collective-permute-start = (bf16[128,2,256]{2,0,1:T(8,128)(2,1)S(1)}, bf16[128,2,256]{2,0,1:T(8,128)(2,1)S(1)}, u32[]{:S(2)}, u32[]{:S(2)}) collective-permute-start(bf16[128,2,256]{2,0,1:T(8,128)(2,1)S(1)} %copy.18), channel_id=1, source_target_pairs={{0,8},{2,10},{4,12},{6,14},{8,16},{10,18},{12,20},{14,22},{16,24},... | collective-permute-start | bytes 393224 | tf_op jit(solution)/shard_map/ppermute | solution.py:21
  5.9 3.4 %collective-permute-start.1 = (bf16[128,2,256]{2,0,1:T(8,128)(2,1)S(1)}, bf16[128,2,256]{2,0,1:T(8,128)(2,1)S(1)}, u32[]{:S(2)}, u32[]{:S(2)}) collective-permute-start(bf16[128,2,256]{2,0,1:T(8,128)(2,1)S(1)} %copy.18), channel_id=1, source_target_pairs={{0,4},{2,6},{4,8},{6,10},{8,12},{10,14},{12,16},{14,18},{16,20},{1... | collective-permute-start | bytes 393224 | tf_op jit(solution)/shard_map/ppermute | solution.py:21
  9.3 0.6 %copy-done.4 = s32[2]{0:T(128)S(1)} copy-done((s32[2]{0:T(128)S(1)}, s32[2]{0:T(128)}, u32[]{:S(2)}) %copy-start.4) | copy-done | bytes 32
  10.0 0.6 %dynamic_slice.3 = s32[1]{0:T(128)} dynamic-slice(s32[2]{0:T(128)S(1)} %copy-done.4, s32[]{:T(128)S(6)} %select_n.67), dynamic_slice_sizes={1} | dynamic-slice | bytes 12 | tf_op jit(solution)/shard_map/dynamic_slice | solution.py:49
  12.5 0.0 copy-start.3
  12.6 0.6 %copy-done.3 = s32[128]{0:T(128)S(1)} copy-done((s32[128]{0:T(128)S(1)}, s32[128]{0:T(128)}, u32[]{:S(2)}) %copy-start.3) | copy-done | bytes 536
  13.2 0.3 fusion.1
  13.5 0.8 %rev.3 = bf16[2,128,512]{2,1,0:T(8,128)(2,1)S(1)} reverse(bf16[2,128,512]{2,1,0:T(8,128)(2,1)S(1)} %fusion.1), dimensions={2} | reverse | bytes 524288 | tf_op jit(solution)/shard_map/rev | solution.py:29
  14.3 0.2 pad.4
  14.5 1.1 %reshape.17 = bf16[2,82048]{1,0:T(2,128)(2,1)S(1)} reshape(bf16[2,128,641]{2,1,0:T(8,128)(2,1)S(1)} %pad.4) | data formatting | bytes 656384 | tf_op jit(solution)/shard_map/reshape | solution.py:32
  15.5 0.2 slice.32
  15.8 0.0 copy-start.5
  15.9 0.6 %copy-done.5 = s32[128]{0:T(128)S(1)} copy-done((s32[128]{0:T(128)S(1)}, s32[128]{0:T(128)}, u32[]{:S(2)}) %copy-start.5) | copy-done | bytes 536
  16.4 0.3 copy-done.1
  16.7 0.2 fusion.14
  16.9 0.1 collective-permute-start.3
  17.0 0.5 %collective-permute-start.2 = (bf16[128,2,256]{2,0,1:T(8,128)(2,1)S(1)}, bf16[128,2,256]{2,0,1:T(8,128)(2,1)S(1)}, u32[]{:S(2)}, u32[]{:S(2)}) collective-permute-start(bf16[128,2,256]{2,0,1:T(8,128)(2,1)S(1)} %get-tuple-element.7), channel_id=1, source_target_pairs={{0,2},{2,0},{4,6},{6,4},{8,10},{10,8},{12,14},{14,12},{16,18},{18,... | collective-permute-start | bytes 393224 | tf_op jit(solution)/shard_map/ppermute | solution.py:24
  17.5 0.2 fusion.18
  17.7 0.7 %collective-permute-done.3 = bf16[128,2,256]{2,0,1:T(8,128)(2,1)S(1)} collective-permute-done((bf16[128,2,256]{2,0,1:T(8,128)(2,1)S(1)}, bf16[128,2,256]{2,0,1:T(8,128)(2,1)S(1)}, u32[]{:S(2)}, u32[]{:S(2)}) %collective-permute-start.3) | collective-permute-done | bytes 131104 | tf_op jit(solution)/shard_map/ppermute | solution.py:24
  18.3 0.2 fusion.16
  18.5 0.0 collective-permute-done.2
  18.5 0.2 fusion.20
  18.7 0.2 fusion.5
  18.9 1.6 %collective-permute-start.4 = (bf16[2,128,256]{2,1,0:T(8,128)(2,1)S(1)}, bf16[2,128,256]{2,1,0:T(8,128)(2,1)S(1)}, u32[]{:S(2)}, u32[]{:S(2)}) collective-permute-start(bf16[2,128,256]{2,1,0:T(8,128)(2,1)S(1)} %fusion.5), channel_id=1, source_target_pairs={{1,0},{0,1},{3,2},{2,3},{5,4},{4,5},{7,6},{6,7},{9,8},{8,9},{11,10... | collective-permute-start | bytes 393224 | tf_op jit(solution)/shard_map/ppermute | solution.py:48
  20.5 4.2 %collective-permute-done.4 = bf16[2,128,256]{2,1,0:T(8,128)(2,1)S(1)} collective-permute-done((bf16[2,128,256]{2,1,0:T(8,128)(2,1)S(1)}, bf16[2,128,256]{2,1,0:T(8,128)(2,1)S(1)}, u32[]{:S(2)}, u32[]{:S(2)}) %collective-permute-start.4) | collective-permute-done | bytes 131104 | tf_op jit(solution)/shard_map/ppermute | solution.py:48
  24.7 0.3 fusion
  25.1 0.1 collective-permute-start.5
  25.2 1.5 %collective-permute-done.5 = f32[8,32,256]{2,1,0:T(8,128)S(1)} collective-permute-done((f32[8,32,256]{2,1,0:T(8,128)S(1)}, f32[8,32,256]{2,1,0:T(8,128)S(1)}, u32[]{:S(2)}, u32[]{:S(2)}) %collective-permute-start.5) | collective-permute-done | bytes 262176 | tf_op jit(solution)/shard_map/ppermute | solution.py:66
  26.7 0.1 fusion.10
  26.8 12.9 %all_to_all.5 = f32[8,32,256]{2,1,0:T(8,128)S(1)} all-to-all(f32[8,32,256]{2,1,0:T(8,128)S(1)} %fusion.10), channel_id=1, replica_groups={{0,4,8,12,16,20,24,28},{2,6,10,14,18,22,26,30},{1,5,9,13,17,21,25,29},{..., dimensions={0} | all-to-all | bytes 524288 | tf_op jit(solution)/shard_map/all_to_all | solution.py:68
  39.6 0.6 %reduce_sum.9 = f32[32,256]{1,0:T(8,128)} reduce(f32[8,32,256]{2,1,0:T(8,128)S(1)} %all_to_all.5, f32[]{:T(128)} %constant.32.clone.1), dimensions={0}, to_apply=%region_0.1 | reduce | flops 57344 | bytes 294916 | tf_op jit(solution)/shard_map/reduce_sum | solution.py:68
  (14 shorter events, 0.2 us)
Async XLA Ops:
  0.0 12.5 %copy-start = (bf16[16,2,512]{2,1,0:T(2,128)(2,1)S(1)}, bf16[16,2,512]{2,1,0:T(2,128)(2,1)}, u32[]{:S(2)}) copy-start(bf16[16,2,512]{2,1,0:T(2,128)(2,1)} %param.7) | copy-start | bytes 98308
  0.9 15.9 %collective-permute-start = (bf16[128,2,256]{2,0,1:T(8,128)(2,1)S(1)}, bf16[128,2,256]{2,0,1:T(8,128)(2,1)S(1)}, u32[]{:S(2)}, u32[]{:S(2)}) collective-permute-start(bf16[128,2,256]{2,0,1:T(8,128)(2,1)S(1)} %copy.18), channel_id=1, source_target_pairs={{0,8},{2,10},{4,12},{6,14},{8,16},{10,18},{12,20},{14,22},{16,24},... | collective-permute-start | bytes 393224 | tf_op jit(solution)/shard_map/ppermute | solution.py:21
  5.9 11.0 %collective-permute-start.1 = (bf16[128,2,256]{2,0,1:T(8,128)(2,1)S(1)}, bf16[128,2,256]{2,0,1:T(8,128)(2,1)S(1)}, u32[]{:S(2)}, u32[]{:S(2)}) collective-permute-start(bf16[128,2,256]{2,0,1:T(8,128)(2,1)S(1)} %copy.18), channel_id=1, source_target_pairs={{0,4},{2,6},{4,8},{6,10},{8,12},{10,14},{12,16},{14,18},{16,20},{1... | collective-permute-start | bytes 393224 | tf_op jit(solution)/shard_map/ppermute | solution.py:21
  9.3 0.7 %copy-start.4 = (s32[2]{0:T(128)S(1)}, s32[2]{0:T(128)}, u32[]{:S(2)}) copy-start(s32[2]{0:T(128)} %param.11) | copy-start | bytes 28
  12.5 0.7 %copy-start.3 = (s32[128]{0:T(128)S(1)}, s32[128]{0:T(128)}, u32[]{:S(2)}) copy-start(s32[128]{0:T(128)} %param.8) | copy-start | bytes 1540
  15.8 0.7 %copy-start.5 = (s32[128]{0:T(128)S(1)}, s32[128]{0:T(128)}, u32[]{:S(2)}) copy-start(s32[128]{0:T(128)} %param.9) | copy-start | bytes 1540
  15.8 0.9 %copy-start.1 = (bf16[128,2,256]{2,1,0:T(2,128)(2,1)S(1)}, bf16[128,2,256]{2,1,0:T(2,128)(2,1)}, u32[]{:S(2)}) copy-start(bf16[128,2,256]{2,1,0:T(2,128)(2,1)} %param.6) | copy-start | bytes 393220
  16.9 1.4 %collective-permute-start.3 = (bf16[128,2,256]{2,0,1:T(8,128)(2,1)S(1)}, bf16[128,2,256]{2,0,1:T(8,128)(2,1)S(1)}, u32[]{:S(2)}, u32[]{:S(2)}) collective-permute-start(bf16[128,2,256]{2,0,1:T(8,128)(2,1)S(1)} %get-tuple-element.8), channel_id=1, source_target_pairs={{0,2},{2,0},{4,6},{6,4},{8,10},{10,8},{12,14},{14,12},{16,18},{18,... | collective-permute-start | bytes 393224 | tf_op jit(solution)/shard_map/ppermute | solution.py:24
  17.0 1.5 %collective-permute-start.2 = (bf16[128,2,256]{2,0,1:T(8,128)(2,1)S(1)}, bf16[128,2,256]{2,0,1:T(8,128)(2,1)S(1)}, u32[]{:S(2)}, u32[]{:S(2)}) collective-permute-start(bf16[128,2,256]{2,0,1:T(8,128)(2,1)S(1)} %get-tuple-element.7), channel_id=1, source_target_pairs={{0,2},{2,0},{4,6},{6,4},{8,10},{10,8},{12,14},{14,12},{16,18},{18,... | collective-permute-start | bytes 393224 | tf_op jit(solution)/shard_map/ppermute | solution.py:24
  18.7 1.8 %copy-start.2 = (f32[2,128]{1,0:T(2,128)S(1)}, f32[2,128]{1,0:T(2,128)}, u32[]{:S(2)}) copy-start(f32[2,128]{1,0:T(2,128)} %param.10) | copy-start | bytes 3076
  18.9 5.8 %collective-permute-start.4 = (bf16[2,128,256]{2,1,0:T(8,128)(2,1)S(1)}, bf16[2,128,256]{2,1,0:T(8,128)(2,1)S(1)}, u32[]{:S(2)}, u32[]{:S(2)}) collective-permute-start(bf16[2,128,256]{2,1,0:T(8,128)(2,1)S(1)} %fusion.5), channel_id=1, source_target_pairs={{1,0},{0,1},{3,2},{2,3},{5,4},{4,5},{7,6},{6,7},{9,8},{8,9},{11,10... | collective-permute-start | bytes 393224 | tf_op jit(solution)/shard_map/ppermute | solution.py:48
  25.1 1.6 %collective-permute-start.5 = (f32[8,32,256]{2,1,0:T(8,128)S(1)}, f32[8,32,256]{2,1,0:T(8,128)S(1)}, u32[]{:S(2)}, u32[]{:S(2)}) collective-permute-start(f32[8,32,256]{2,1,0:T(8,128)S(1)} %select_bitcast_fusion), channel_id=1, source_target_pairs={{0,2},{2,0},{4,6},{6,4},{8,10},{10,8},{12,14},{14,12},{16,18},{18,... | collective-permute-start | bytes 786440 | tf_op jit(solution)/shard_map/ppermute | solution.py:66

commit v2 on v1

v2 whole, which is shorter than its diff:
```python
import functools

import jax
import jax.numpy as jnp
from jax import lax
from jax.experimental import pallas as pl
from jax.experimental.pallas import tpu as pltpu
from jax.sharding import PartitionSpec as P

VMEM = pl.BlockSpec(memory_space=pltpu.VMEM)
SMEM = pl.BlockSpec(memory_space=pltpu.SMEM)
FIRST = (((0,), (0,)), ((), ()))
LIMIT = pltpu.CompilerParams(vmem_limit_bytes=24 * 2**20)


def toeplitz_kernel(segment_ref, taps_ref, weights_ref, flags_ref, design_ref, out_ref, row_weight_ref, own_ref):
    own_ref[...] = design_ref[...]
    seg_count = taps_ref.shape[0] // 2
    tap_count = taps_ref.shape[1]
    row_count = segment_ref.shape[1]
    width = out_ref.shape[1]
    halo_rows = width // 2 - row_count
    tile = 128
    tiles = tap_count // tile
    lane = lax.broadcasted_iota(jnp.int32, (tile, 2 * tile), 1)
    row = lax.broadcasted_iota(jnp.int32, (tile, 2 * tile), 0)
    flip = (lane == 2 * (tile - 1 - row)).astype(jnp.float32).astype(jnp.bfloat16)
    seg = lax.broadcasted_iota(jnp.int32, (seg_count, row_count), 0)
    selector = (seg == segment_ref[...]).astype(jnp.float32).astype(jnp.bfloat16)
    column = lax.broadcasted_iota(jnp.int32, (row_count, width), 1)
    first_column = 2 * (halo_rows - lax.axis_index("tm") * row_count)
    row_weight = weights_ref[...] * flags_ref[...].astype(jnp.float32)
    for k in range(2):
        taps = taps_ref[k * seg_count : (k + 1) * seg_count, :]
        pieces = [
            jnp.dot(taps[:, m * tile : (m + 1) * tile], flip, preferred_element_type=jnp.float32)
            for m in range(tiles - 1, -1, -1)
        ]
        pieces.append(jnp.zeros((seg_count, width - 2 * tap_count), jnp.float32))
        spread = pltpu.roll(jnp.concatenate(pieces, axis=1), 2 * (halo_rows - tap_count + 1) + k, 1)
        rows = lax.dot_general(selector, spread.astype(jnp.bfloat16), FIRST, preferred_element_type=jnp.float32)
        rows = pltpu.roll(rows, 0, 1, stride=2, stride_axis=0)
        rows = jnp.where(column >= first_column, rows, 0.0)
        out_ref[k * row_count : (k + 1) * row_count, :] = rows.astype(jnp.bfloat16)
        row_weight_ref[k * row_count : (k + 1) * row_count, :] = jnp.broadcast_to(
            row_weight[k : k + 1, :], (tile, row_count)
        ).T


def filter_kernel(toeplitz_ref, *refs):
    *block_refs, out_ref = refs
    row_count, _, width = block_refs[0].shape
    step = 2 * row_count
    total = None
    for j, block_ref in enumerate(block_refs):
        product = jnp.dot(
            toeplitz_ref[:, j * step : (j + 1) * step],
            block_ref[...].reshape(step, width),
            preferred_element_type=jnp.float32,
        )
        total = product if total is None else total + product
    out_ref[...] = total.astype(jnp.bfloat16)


def gram_kernel(ids_ref, row_weight_ref, *refs):
    *held_refs, mine_ref, other_ref, scaled_ref = refs
    columns = len(held_refs)
    width = held_refs[0].shape[1]
    rows_out = mine_ref.shape[1]
    pairs = width // rows_out // 2
    parity = lax.rem(lax.axis_index("tm"), 2)
    column = lax.axis_index("col")
    ids = [ids_ref[lax.rem(column + d, columns)] for d in range(columns)]
    for d in range(columns):

        @pl.when(ids[d] == column)
        def _(d=d):
            weight = jnp.concatenate([row_weight_ref[...]] * (width // row_weight_ref.shape[1]), axis=1)
            scaled_ref[...] = (held_refs[d][...].astype(jnp.float32) * weight).astype(jnp.bfloat16)

    for d in range(columns):
        product = lax.dot_general(
            held_refs[d][...], scaled_ref[...], FIRST, preferred_element_type=jnp.float32
        ).reshape(pairs, 2, rows_out, width)
        for own in range(2):

            @pl.when(parity == own)
            def _(d=d, own=own, product=product):
                place = pl.ds(ids[d] * pairs, pairs)
                mine_ref[place] = product[:, own]
                other_ref[place] = product[:, 1 - own]


def body(design, filter_taps, segment, valid_flags, weights, block_ids):
    row_count = design.shape[0]
    block_width = design.shape[2]
    tap_count = filter_taps.shape[2]
    seg_count = filter_taps.shape[0]
    devices = lax.axis_size("tm")
    columns = lax.axis_size("col")
    chips = devices // 2
    rows_out = columns * block_width // devices
    halo_depth = (tap_count - 2) // row_count + 1
    index = lax.axis_index("tm")
    odd = index % 2 == 1
    swap = [(i, i ^ 1) for i in range(devices)]

    blocks = [design] + [None] * halo_depth
    for hop in range(2, halo_depth + 1, 2):
        blocks[hop] = lax.ppermute(design, "tm", [(i, (i + hop) % devices) for i in range(devices)])
    toeplitz, row_weight, blocks[0] = pl.pallas_call(
        toeplitz_kernel,
        out_shape=[
            jax.ShapeDtypeStruct((2 * row_count, 2 * (halo_depth + 1) * row_count), jnp.bfloat16),
            jax.ShapeDtypeStruct((2 * row_count, 128), jnp.float32),
            jax.ShapeDtypeStruct(design.shape, design.dtype),
        ],
        in_specs=[VMEM] * 5,
        out_specs=[VMEM] * 3,
        compiler_params=LIMIT,
        name="toeplitz",
    )(
        segment.reshape(1, row_count),
        filter_taps.transpose(1, 0, 2).reshape(2 * seg_count, tap_count),
        weights,
        valid_flags.reshape(1, row_count),
        design,
    )
    for hop in range(1, halo_depth + 1, 2):
        blocks[hop] = lax.ppermute(jnp.where(odd, blocks[hop + 1], blocks[hop - 1]), "tm", swap)
    filtered = pl.pallas_call(
        filter_kernel,
        out_shape=jax.ShapeDtypeStruct((2 * row_count, block_width), jnp.bfloat16),
        in_specs=[VMEM] * (halo_depth + 2),
        out_specs=VMEM,
        compiler_params=LIMIT,
        name="filter",
    )(toeplitz, *blocks[::-1])

    held = [filtered]
    for d in range(1, columns):
        held.append(lax.ppermute(filtered, "col", [((c + d) % columns, c) for c in range(columns)]))
    half = jax.ShapeDtypeStruct((chips, rows_out, block_width), jnp.float32)
    mine, other = pl.pallas_call(
        gram_kernel,
        out_shape=[half, half],
        in_specs=[SMEM] + [VMEM] * (1 + columns),
        out_specs=[VMEM] * 2,
        scratch_shapes=[pltpu.VMEM((2 * row_count, block_width), jnp.bfloat16)],
        compiler_params=LIMIT,
        name="gram",
    )(block_ids, row_weight, *held)

    total = mine + lax.ppermute(other, "tm", swap)
    stride, left = 2, chips
    while left > 1:
        group = 4 if left % 4 == 0 else 2
        shares = total.reshape(left // group, group, rows_out, block_width)
        place = index // stride % group

        def share(j):
            return lax.dynamic_index_in_dim(shares, j, 1, keepdims=False)

        total = share(place)
        for d in (3, 1, 2)[-(group - 1) :] if group == 4 else (1,):
            total = total + lax.ppermute(share(place ^ d), "tm", [(i, i ^ (d * stride)) for i in range(devices)])
        stride, left = stride * group, left // group
    return total[0] * (1.0 / (2.0 * row_count * devices))


def solution(mesh):
    return jax.shard_map(
        body,
        mesh=mesh,
        in_specs=(P("tm", None, "col"), P(), P("tm"), P("tm"), P(None, "tm"), P()),
        out_specs=P("tm", "col"),
        check_vma=False,
    )
```

time: 40.5 us -> 34.7 us (0.86)
  blocking collectives: 12.9 us -> 0 us
  waiting for transfers between devices: 6.43 us -> 16.5 us
  local copies, waits for them, and re-layouts: 5.99 us -> 2.39 us
  Pallas kernels: 0 us -> 2.36 us
  between operations: 2.2 us -> 0.16 us
  starting transfers between devices: 10.6 us -> 12.4 us
  matrix products: 1.44 us -> 0 us
    all_to_all x1 -> x0, blocking collectives: 12.9 us -> none  [body(): return lax.all_to_all(mine, 'tm', 0, 0, axis_index_groups=groups).sum(0)]
    ppermute x5 -> x9, waiting for transfers between devices: 2.2 us -> 12.3 us  [the longest x4 5.05 us: body(): lax.ppermute(share(place ^ d), 'tm', [(i, i ^ d * stride) for i in range(...]
    pallas_call x0 -> x3, Pallas kernels: none -> 2.36 us  [the longest x1 1.06 us: body(): pl.pallas_call(gram_kernel, out_shape=[half, half], in_specs=[SMEM] + [VM...]
    ppermute x5 -> x9, starting transfers between devices: 9.01 us -> 10.8 us  [the longest x4 5.62 us: body(): lax.ppermute(share(place ^ d), 'tm', [(i, i ^ d * stride) for i in range(...]
    unnamed x14 -> x10, local copies, waits for them, and re-layouts: 3.12 us -> 1.59 us
    dot_general x7 -> x0, matrix products: 1.44 us -> none  [the longest x5 0.85 us: body(): jnp.einsum('kts,skc->ktc', toeplitz[:, :, (halo_depth - d) * row_count:(h...]
    reshape x1 -> x0, local copies, waits for them, and re-layouts: 1.06 us -> none  [body(): padded.reshape(2, row_count * (window_rows + 1))]
    rev x1 -> x0, local copies, waits for them, and re-layouts: 0.84 us -> none  [body(): reversed_taps = tap_rows[:, :, ::-1]]
  transfers between devices with their start and end apart: 6 -> 10, of which waited for: 3 -> 10; matrix products, arithmetic and copies ran while one was open for 9% -> 2% of each run, Pallas kernels for 0% -> 3%
where the time goes in v2:
time: 34.7 us; the launch traced here: 34.5 us
  waiting for transfers between devices  16.5 us (48%)
  starting transfers between devices  12.4 us (36%)
  local copies, waits for them, and re-layouts  2.39 us (7%)
  Pallas kernels  2.36 us (7%)
  other arithmetic  0.7 us (2%)
    ppermute x4, starting transfers between devices, body(): lax.ppermute(share(place ^ d), 'tm', [(i, i ^ d * stride) for i in range(...  5.62 us
    ppermute x4, waiting for transfers between devices, body(): lax.ppermute(share(place ^ d), 'tm', [(i, i ^ d * stride) for i in range(...  5.05 us
    ppermute x2, waiting for transfers between devices, body(): lax.ppermute(design, 'tm', [(i, (i + hop) % devices) for i in range(devic...  4.73 us
    ppermute x2, starting transfers between devices, body(): lax.ppermute(design, 'tm', [(i, (i + hop) % devices) for i in range(devic...  4.54 us
    ppermute x1, waiting for transfers between devices, body(): lax.ppermute(filtered, 'col', [((c + d) % columns, c) for c in range(colu...  4.23 us
    unnamed x10, local copies, waits for them, and re-layouts  1.59 us
    ppermute x1, starting transfers between devices, body(): lax.ppermute(filtered, 'col', [((c + d) % columns, c) for c in range(colu...  1.56 us
    ppermute x1, waiting for transfers between devices, body(): total = mine + lax.ppermute(other, 'tm', swap)  1.47 us
  transfers between devices with their start and end apart: 10, of which 10 were waited for; matrix products, arithmetic and copies ran while one was open for 2% of the time, Pallas kernels for 3%

profile of v2, /device:TPU:0, one launch (start us, length us, event | category | flops | bytes accessed | tf_op | source)
XLA Modules:
  0.0 34.5 jit_solution(18192837395405023759)
XLA Ops:
  0.0 3.0 %collective-permute-start = (bf16[128,2,256]{2,1,0:T(2,128)(2,1)}, bf16[128,2,256]{2,1,0:T(2,128)(2,1)S(1)}, u32[]{:S(2)}, u32[]{:S(2)}) collective-permute-start(bf16[128,2,256]{2,1,0:T(2,128)(2,1)} %design_ref.1), channel_id=1, source_target_pairs={{0,8},{2,10},{4,12},{6,14},{8,16},{10,18},{12,20},{14,22},{16,24},... | collective-permute-start | bytes 393224 | tf_op jit(solution)/shard_map/ppermute | solution.py:110
  3.0 1.5 %collective-permute-start.1 = (bf16[128,2,256]{2,1,0:T(2,128)(2,1)}, bf16[128,2,256]{2,1,0:T(2,128)(2,1)S(1)}, u32[]{:S(2)}, u32[]{:S(2)}) collective-permute-start(bf16[128,2,256]{2,1,0:T(2,128)(2,1)} %design_ref.1), channel_id=1, source_target_pairs={{0,4},{2,6},{4,8},{6,10},{8,12},{10,14},{12,16},{14,18},{16,20},{1... | collective-permute-start | bytes 393224 | tf_op jit(solution)/shard_map/ppermute | solution.py:110
  4.5 0.8 %copy.7 = bf16[2,16,512]{2,1,0:T(8,128)(2,1)S(1)} copy(bf16[2,16,512]{2,0,1:T(2,128)(2,1)} %bitcast.34) | data formatting | bytes 65536 | tf_op jit(solution)/shard_map/transpose | solution.py:124
  5.3 0.0 copy-start.3
  5.3 0.6 %copy-done.4 = s32[128]{0:T(128)S(1)} copy-done((s32[128]{0:T(128)S(1)}, s32[128]{0:T(128)}, u32[]{:S(2)}) %copy-start.4) | copy-done | bytes 536
  6.0 0.0 copy-done.1
  6.0 0.0 copy-done.3
  6.0 0.9 %copy-done = bf16[128,2,256]{2,1,0:T(2,128)(2,1)S(1)} copy-done((bf16[128,2,256]{2,1,0:T(2,128)(2,1)S(1)}, bf16[128,2,256]{2,1,0:T(2,128)(2,1)}, u32[]{:S(2)}) %copy-start) | copy-done | bytes 131096
  6.9 0.9 %toeplitz.1 = (bf16[256,1280]{1,0:T(8,128)(2,1)S(1)}, f32[256,128]{1,0:T(8,128)S(1)}, bf16[128,2,256]{2,1,0:T(2,128)(2,1)S(1)}) custom-call(s32[1,128]{1,0:T(1,128)S(1)} %bitcast.28, bf16[32,512]{1,0:T(8,128)(2,1)S(1)} %bitcast.27, f32[2,128]{1,0:T(2,128)S(1)} %copy-done.1, s32[1,128]{1,0:T(1,128)S(1)} %bitcast.29, bf16[128,2,256]{2,1,0:T(2,128)(2,1)S(1)} %copy-done), custom_call_target="tpu_custom_call" | custom-call | tf_op jit(solution)/shard_map/toeplitz/pallas_call | solution.py:111
  7.8 1.0 %collective-permute-done.refs_0_ = bf16[128,2,256]{2,1,0:T(2,128)(2,1)S(1)} collective-permute-done((bf16[128,2,256]{2,1,0:T(2,128)(2,1)}, bf16[128,2,256]{2,1,0:T(2,128)(2,1)S(1)}, u32[]{:S(2)}, u32[]{:S(2)}) %collective-permute-start) | collective-permute-done | bytes 131104 | tf_op jit(solution)/shard_map/ppermute | solution.py:110
  8.8 3.8 %collective-permute-done.1.refs_2_ = bf16[128,2,256]{2,1,0:T(2,128)(2,1)S(1)} collective-permute-done((bf16[128,2,256]{2,1,0:T(2,128)(2,1)}, bf16[128,2,256]{2,1,0:T(2,128)(2,1)S(1)}, u32[]{:S(2)}, u32[]{:S(2)}) %collective-permute-start.1) | collective-permute-done | bytes 131104 | tf_op jit(solution)/shard_map/ppermute | solution.py:110
  12.5 0.1 collective-permute-start.2
  12.6 0.5 %collective-permute-start.3 = (bf16[128,2,256]{2,1,0:T(2,128)(2,1)S(1)}, bf16[128,2,256]{2,1,0:T(2,128)(2,1)S(1)}, u32[]{:S(2)}, u32[]{:S(2)}) collective-permute-start(bf16[128,2,256]{2,1,0:T(2,128)(2,1)S(1)} %bitcast.32), channel_id=1, source_target_pairs={{0,2},{2,0},{4,6},{6,4},{8,10},{10,8},{12,14},{14,12},{16,18},{18,... | collective-permute-start | bytes 393224 | tf_op jit(solution)/shard_map/ppermute | solution.py:130
  13.1 0.8 %collective-permute-done.2.refs_1_ = bf16[128,2,256]{2,1,0:T(2,128)(2,1)S(1)} collective-permute-done((bf16[128,2,256]{2,1,0:T(2,128)(2,1)S(1)}, bf16[128,2,256]{2,1,0:T(2,128)(2,1)S(1)}, u32[]{:S(2)}, u32[]{:S(2)}) %collective-permute-start.2) | collective-permute-done | bytes 131104 | tf_op jit(solution)/shard_map/ppermute | solution.py:130
  14.0 0.2 collective-permute-done.3.refs_3_
  14.1 0.4 %filter.1.refs_0_ = bf16[256,256]{1,0:T(8,128)(2,1)S(1)} custom-call(bf16[256,1280]{1,0:T(8,128)(2,1)S(1)} %get-tuple-element.11.toeplitz_ref, bf16[128,2,256]{2,1,0:T(2,128)(2,1)S(1)} %collective-permute-done.refs_0_, bf16[128,2,256]{2,1,0:T(2,128)(2,1)S(1)} %collective-permute-done.2.refs_1_, bf16[128,2,256]{2,1,0:T(2,128)(2,1)S(1)} %collective-permute-done.1.refs_2_, ...), custom_call_target="tpu_custom_call" | custom-call | tf_op jit(solution)/shard_map/filter/pallas_call | solution.py:131
  14.6 0.0 copy-start.2
  14.6 1.6 %collective-permute-start.4 = (bf16[256,256]{1,0:T(8,128)(2,1)S(1)}, bf16[256,256]{1,0:T(8,128)(2,1)S(1)}, u32[]{:S(2)}, u32[]{:S(2)}) collective-permute-start(bf16[256,256]{1,0:T(8,128)(2,1)S(1)} %filter.1.refs_0_), channel_id=1, source_target_pairs={{1,0},{0,1},{3,2},{2,3},{5,4},{4,5},{7,6},{6,7},{9,8},{8,9},{11,10... | collective-permute-start | bytes 393224 | tf_op jit(solution)/shard_map/ppermute | solution.py:142
  16.1 4.2 %collective-permute-done.4.refs_1_ = bf16[256,256]{1,0:T(8,128)(2,1)S(1)} collective-permute-done((bf16[256,256]{1,0:T(8,128)(2,1)S(1)}, bf16[256,256]{1,0:T(8,128)(2,1)S(1)}, u32[]{:S(2)}, u32[]{:S(2)}) %collective-permute-start.4) | collective-permute-done | bytes 131104 | tf_op jit(solution)/shard_map/ppermute | solution.py:142
  20.4 0.0 copy-done.2
  20.4 1.1 %gram.1 = (f32[8,32,256]{2,1,0:T(8,128)S(1)}, f32[8,32,256]{2,1,0:T(8,128)S(1)}) custom-call(s32[2]{0:T(128)S(1)} %copy-done.2, f32[256,128]{1,0:T(8,128)S(1)} %get-tuple-element.10.row_weight_ref, bf16[256,256]{1,0:T(8,128)(2,1)S(1)} %filter.1.refs_0_, bf16[256,256]{1,0:T(8,128)(2,1)S(1)} %collective-permute-done.4.refs_1_), custom_call_target="tpu_custom_call" | custom-call | tf_op jit(solution)/shard_map/gram/pallas_call | solution.py:144
  21.4 0.1 collective-permute-start.5
  21.6 1.5 %collective-permute-done.5 = f32[8,32,256]{2,1,0:T(8,128)S(1)} collective-permute-done((f32[8,32,256]{2,1,0:T(8,128)S(1)}, f32[8,32,256]{2,1,0:T(8,128)S(1)}, u32[]{:S(2)}, u32[]{:S(2)}) %collective-permute-start.5) | collective-permute-done | bytes 262176 | tf_op jit(solution)/shard_map/ppermute | solution.py:154
  23.1 0.1 collective-permute-start.8
  23.2 0.1 collective-permute-start.7
  23.3 3.4 %collective-permute-start.6 = (f32[2,32,256]{2,1,0:T(8,128)S(1)}, f32[2,32,256]{2,1,0:T(8,128)S(1)}, u32[]{:S(2)}, u32[]{:S(2)}) collective-permute-start(f32[2,32,256]{2,1,0:T(8,128)S(1)} %get-tuple-element.15), channel_id=1, source_target_pairs={{0,12},{2,14},{4,8},{6,10},{8,4},{10,6},{12,0},{14,2},{16,28},{18,... | collective-permute-start | bytes 196616 | tf_op jit(solution)/shard_map/ppermute | solution.py:166
  26.7 1.1 %collective-permute-done.8 = f32[2,32,256]{2,1,0:T(8,128)S(1)} collective-permute-done((f32[2,32,256]{2,1,0:T(8,128)S(1)}, f32[2,32,256]{2,1,0:T(8,128)S(1)}, u32[]{:S(2)}, u32[]{:S(2)}) %collective-permute-start.8) | collective-permute-done | bytes 65568 | tf_op jit(solution)/shard_map/ppermute | solution.py:166
  27.8 0.6 %collective-permute-done.7 = f32[2,32,256]{2,1,0:T(8,128)S(1)} collective-permute-done((f32[2,32,256]{2,1,0:T(8,128)S(1)}, f32[2,32,256]{2,1,0:T(8,128)S(1)}, u32[]{:S(2)}, u32[]{:S(2)}) %collective-permute-start.7) | collective-permute-done | bytes 65568 | tf_op jit(solution)/shard_map/ppermute | solution.py:166
  28.4 0.6 %collective-permute-done.6 = f32[2,32,256]{2,1,0:T(8,128)S(1)} collective-permute-done((f32[2,32,256]{2,1,0:T(8,128)S(1)}, f32[2,32,256]{2,1,0:T(8,128)S(1)}, u32[]{:S(2)}, u32[]{:S(2)}) %collective-permute-start.6) | collective-permute-done | bytes 65568 | tf_op jit(solution)/shard_map/ppermute | solution.py:166
  29.0 2.1 %collective-permute-start.9 = (f32[1,32,256]{2,1,0:T(8,128)S(1)}, f32[1,32,256]{2,1,0:T(8,128)S(1)}, u32[]{:S(2)}, u32[]{:S(2)}) collective-permute-start(f32[1,32,256]{2,1,0:T(8,128)S(1)} %constant_dynamic-slice_fusion), channel_id=1, source_target_pairs={{0,16},{2,18},{4,20},{6,22},{8,24},{10,26},{12,28},{14,30},{16,0},... | collective-permute-start | bytes 98312 | tf_op jit(solution)/shard_map/ppermute | solution.py:166
  31.1 2.8 %collective-permute-done.9 = f32[1,32,256]{2,1,0:T(8,128)S(1)} collective-permute-done((f32[1,32,256]{2,1,0:T(8,128)S(1)}, f32[1,32,256]{2,1,0:T(8,128)S(1)}, u32[]{:S(2)}, u32[]{:S(2)}) %collective-permute-start.9) | collective-permute-done | bytes 32800 | tf_op jit(solution)/shard_map/ppermute | solution.py:166
  33.9 0.6 %multiply_bitcast_fusion = f32[32,256]{1,0:T(8,128)} fusion(f32[1,32,256]{2,1,0:T(8,128)S(1)} %collective-permute-done.9, f32[2,32,256]{2,1,0:T(8,128)S(1)} %fusion.1, s32[]{:T(128)S(6)} %select_n.66), kind=kLoop, calls=%fused_computation.8 | loop fusion | flops 16384 | bytes 98308 | tf_op jit(solution)/shard_map/mul | solution.py:168
  (8 shorter events, 0.1 us)
Async XLA Ops:
  0.0 8.8 %collective-permute-start = (bf16[128,2,256]{2,1,0:T(2,128)(2,1)}, bf16[128,2,256]{2,1,0:T(2,128)(2,1)S(1)}, u32[]{:S(2)}, u32[]{:S(2)}) collective-permute-start(bf16[128,2,256]{2,1,0:T(2,128)(2,1)} %design_ref.1), channel_id=1, source_target_pairs={{0,8},{2,10},{4,12},{6,14},{8,16},{10,18},{12,20},{14,22},{16,24},... | collective-permute-start | bytes 393224 | tf_op jit(solution)/shard_map/ppermute | solution.py:110
  3.0 9.5 %collective-permute-start.1 = (bf16[128,2,256]{2,1,0:T(2,128)(2,1)}, bf16[128,2,256]{2,1,0:T(2,128)(2,1)S(1)}, u32[]{:S(2)}, u32[]{:S(2)}) collective-permute-start(bf16[128,2,256]{2,1,0:T(2,128)(2,1)} %design_ref.1), channel_id=1, source_target_pairs={{0,4},{2,6},{4,8},{6,10},{8,12},{10,14},{12,16},{14,18},{16,20},{1... | collective-permute-start | bytes 393224 | tf_op jit(solution)/shard_map/ppermute | solution.py:110
  5.3 0.7 %copy-start.4 = (s32[128]{0:T(128)S(1)}, s32[128]{0:T(128)}, u32[]{:S(2)}) copy-start(s32[128]{0:T(128)} %param.9) | copy-start | bytes 1540
  5.3 0.7 %copy-start.1 = (f32[2,128]{1,0:T(2,128)S(1)}, f32[2,128]{1,0:T(2,128)}, u32[]{:S(2)}) copy-start(f32[2,128]{1,0:T(2,128)} %weights_ref.1) | copy-start | bytes 3076
  5.3 0.7 %copy-start.3 = (s32[128]{0:T(128)S(1)}, s32[128]{0:T(128)}, u32[]{:S(2)}) copy-start(s32[128]{0:T(128)} %param.8) | copy-start | bytes 1540
  6.0 0.9 %copy-start = (bf16[128,2,256]{2,1,0:T(2,128)(2,1)S(1)}, bf16[128,2,256]{2,1,0:T(2,128)(2,1)}, u32[]{:S(2)}) copy-start(bf16[128,2,256]{2,1,0:T(2,128)(2,1)} %design_ref.1) | copy-start | bytes 393220
  12.5 1.4 %collective-permute-start.2 = (bf16[128,2,256]{2,1,0:T(2,128)(2,1)S(1)}, bf16[128,2,256]{2,1,0:T(2,128)(2,1)S(1)}, u32[]{:S(2)}, u32[]{:S(2)}) collective-permute-start(bf16[128,2,256]{2,1,0:T(2,128)(2,1)S(1)} %bitcast.33), channel_id=1, source_target_pairs={{0,2},{2,0},{4,6},{6,4},{8,10},{10,8},{12,14},{14,12},{16,18},{18,... | collective-permute-start | bytes 393224 | tf_op jit(solution)/shard_map/ppermute | solution.py:130
  12.6 1.5 %collective-permute-start.3 = (bf16[128,2,256]{2,1,0:T(2,128)(2,1)S(1)}, bf16[128,2,256]{2,1,0:T(2,128)(2,1)S(1)}, u32[]{:S(2)}, u32[]{:S(2)}) collective-permute-start(bf16[128,2,256]{2,1,0:T(2,128)(2,1)S(1)} %bitcast.32), channel_id=1, source_target_pairs={{0,2},{2,0},{4,6},{6,4},{8,10},{10,8},{12,14},{14,12},{16,18},{18,... | collective-permute-start | bytes 393224 | tf_op jit(solution)/shard_map/ppermute | solution.py:130
  14.6 5.8 %copy-start.2 = (s32[2]{0:T(128)S(1)}, s32[2]{0:T(128)}, u32[]{:S(2)}) copy-start(s32[2]{0:T(128)} %ids_ref.1) | copy-start | bytes 28
  14.6 5.8 %collective-permute-start.4 = (bf16[256,256]{1,0:T(8,128)(2,1)S(1)}, bf16[256,256]{1,0:T(8,128)(2,1)S(1)}, u32[]{:S(2)}, u32[]{:S(2)}) collective-permute-start(bf16[256,256]{1,0:T(8,128)(2,1)S(1)} %filter.1.refs_0_), channel_id=1, source_target_pairs={{1,0},{0,1},{3,2},{2,3},{5,4},{4,5},{7,6},{6,7},{9,8},{8,9},{11,10... | collective-permute-start | bytes 393224 | tf_op jit(solution)/shard_map/ppermute | solution.py:142
  21.4 1.6 %collective-permute-start.5 = (f32[8,32,256]{2,1,0:T(8,128)S(1)}, f32[8,32,256]{2,1,0:T(8,128)S(1)}, u32[]{:S(2)}, u32[]{:S(2)}) collective-permute-start(f32[8,32,256]{2,1,0:T(8,128)S(1)} %get-tuple-element.14), channel_id=1, source_target_pairs={{0,2},{2,0},{4,6},{6,4},{8,10},{10,8},{12,14},{14,12},{16,18},{18,... | collective-permute-start | bytes 786440 | tf_op jit(solution)/shard_map/ppermute | solution.py:154
  23.1 4.7 %collective-permute-start.8 = (f32[2,32,256]{2,1,0:T(8,128)S(1)}, f32[2,32,256]{2,1,0:T(8,128)S(1)}, u32[]{:S(2)}, u32[]{:S(2)}) collective-permute-start(f32[2,32,256]{2,1,0:T(8,128)S(1)} %get-tuple-element.16), channel_id=1, source_target_pairs={{0,8},{2,10},{4,12},{6,14},{8,0},{10,2},{12,4},{14,6},{16,24},{18,... | collective-permute-start | bytes 196616 | tf_op jit(solution)/shard_map/ppermute | solution.py:166
  23.2 5.2 %collective-permute-start.7 = (f32[2,32,256]{2,1,0:T(8,128)S(1)}, f32[2,32,256]{2,1,0:T(8,128)S(1)}, u32[]{:S(2)}, u32[]{:S(2)}) collective-permute-start(f32[2,32,256]{2,1,0:T(8,128)S(1)} %get-tuple-element.17), channel_id=1, source_target_pairs={{0,4},{2,6},{4,0},{6,2},{8,12},{10,14},{12,8},{14,10},{16,20},{18,... | collective-permute-start | bytes 196616 | tf_op jit(solution)/shard_map/ppermute | solution.py:166
  23.3 5.7 %collective-permute-start.6 = (f32[2,32,256]{2,1,0:T(8,128)S(1)}, f32[2,32,256]{2,1,0:T(8,128)S(1)}, u32[]{:S(2)}, u32[]{:S(2)}) collective-permute-start(f32[2,32,256]{2,1,0:T(8,128)S(1)} %get-tuple-element.15), channel_id=1, source_target_pairs={{0,12},{2,14},{4,8},{6,10},{8,4},{10,6},{12,0},{14,2},{16,28},{18,... | collective-permute-start | bytes 196616 | tf_op jit(solution)/shard_map/ppermute | solution.py:166
  29.0 4.9 %collective-permute-start.9 = (f32[1,32,256]{2,1,0:T(8,128)S(1)}, f32[1,32,256]{2,1,0:T(8,128)S(1)}, u32[]{:S(2)}, u32[]{:S(2)}) collective-permute-start(f32[1,32,256]{2,1,0:T(8,128)S(1)} %constant_dynamic-slice_fusion), channel_id=1, source_target_pairs={{0,16},{2,18},{4,20},{6,22},{8,24},{10,26},{12,28},{14,30},{16,0},... | collective-permute-start | bytes 98312 | tf_op jit(solution)/shard_map/ppermute | solution.py:166
